TPU v7x, 256 devices: a whole 4x4x8 slice. The times are simulated.
256 devices in a mesh: region: 32 (over y, z_lo, core), factor: 8 (over x, z_hi).
Axes of the slice: x: 4, y: 4, z: 8 (z_hi: 2, z_lo: 4; z = z_hi * 4 + z_lo), core: 2. Of those that a mesh axis runs over, the one named last changes fastest.
Arguments:
- response: bfloat16 [2000, 262144], P('factor', 'region'), may hold values from -6 to 6
- loadings: float32 [2000, 8], replicated, may hold values from -6 to 6
- obs_count: int32 [2000], replicated, may hold values from 1 to 16
- couplings: float32 [8, 2048, 2], P('factor', 'region'), may hold values from 0.3 to 0.9
- block_cov: float32 [8, 2048, 128, 128], P('factor', 'region'), may hold values from -0.07 to 0.5
- noise_factor: float32 [8, 2048, 128, 128], P('factor', 'region'), may hold values from -0.09 to 0.65
- noise: float32 [8, 262144], P('factor', 'region'), may hold values from -6 to 6
- latents: float32 [8, 262144], P('factor', 'region'), may hold values from -6 to 6
- colours: int32 [64], P('region'), may hold values from 0 to 3
- partners: int32 [64, 2], P('region'), may hold values from 0 to 63, as said below
Outputs:
- new_latents: float32 [8, 262144], P('factor', 'region')
Inputs may be any that keep to these rules, and one draw needn't show every extreme that they name: Column 1 of partners is a permutation of the regions, and partners[partners[g, 1], 0] = g for every region g.
All inputs are finite; a program needn't handle non-finite values.
Results may differ from a plain program's by a relative error of at most 0.00088.
Values sent between devices are 32-bit elements; how exact they have to be, the bound alone decides.
A program may use at most 64 MiB of HBM per device.

v0:
```python
from functools import partial
import math

import jax
import jax.numpy as jnp
from jax import lax
from jax.sharding import PartitionSpec as P

COLOURS = 4


exact_mode = lax.Precision.HIGHEST


def apply_blocks(matrices, vectors):
    return jnp.einsum("...ij,...j->...i", matrices, vectors, precision=exact_mode)


def add_cross(own_rows, running, shard_part, first_row):
    return jnp.dot(own_rows, shard_part, precision=exact_mode, preferred_element_type=jnp.float32)


def end_stack(current, block_shape):
    blocks = current.reshape(block_shape)
    per_region = block_shape[2]
    return jnp.stack([blocks[:, :, 0], blocks[:, :, per_region - 1]], axis=2)


def pick_edges(gathered, partners):
    left_edge = jnp.take(gathered[:, :, 1], partners[:, 0], axis=1)
    right_edge = jnp.take(gathered[:, :, 0], partners[:, 1], axis=1)
    return (left_edge, right_edge)


def on_device(
    response,
    loadings,
    obs_count,
    couplings,
    block_cov,
    noise_factor,
    noise,
    latents,
    colours,
    partners,
):
    local_f, sites_dev = latents.shape
    block_width = block_cov.shape[-1]
    regions = colours.shape[0]
    per_region = sites_dev // (regions * block_width)
    block_shape = (local_f, regions, per_region, block_width)
    species_local = response.shape[0]
    factors = loadings.shape[1]
    findex = lax.axis_index("factor")
    weights = obs_count.astype(jnp.float32) * (0.25 / math.sqrt(loadings.shape[0]))
    weighted = loadings * weights[:, None]
    gram_matrix = jnp.dot(weighted.T, loadings, precision=exact_mode)
    offdiag = gram_matrix * (1.0 - jnp.eye(factors, dtype=jnp.float32))
    own_rows = lax.dynamic_slice_in_dim(offdiag, findex * local_f, local_f, 0)
    weighted_local = lax.dynamic_slice_in_dim(
        weighted, findex * species_local, species_local, 0
    ).astype(jnp.bfloat16)
    data_term = lax.psum_scatter(
        jnp.dot(weighted_local.T, response, preferred_element_type=jnp.float32),
        "factor",
        scatter_dimension=0,
        tiled=True,
    )
    coupled = couplings.reshape(local_f, regions, per_region, 2)
    noise_draw = apply_blocks(
        noise_factor, noise.reshape(local_f, regions * per_region, block_width)
    )
    start_total = jnp.zeros((local_f, sites_dev), jnp.float32)
    folder = partial(add_cross, own_rows)
    current = latents
    for phase_index in range(COLOURS):
        cross = folder(
            start_total, lax.all_gather(current, "factor", axis=0, tiled=True), jnp.int32(0)
        )
        gathered = lax.all_gather(end_stack(current, block_shape), "region", axis=1, tiled=True)
        left_edge, right_edge = pick_edges(gathered, partners)
        blocks = current.reshape(block_shape)
        left_block = jnp.concatenate([left_edge[:, :, None], blocks[:, :, :-1]], axis=2)
        right_block = jnp.concatenate([blocks[:, :, 1:], right_edge[:, :, None]], axis=2)
        field_term = (data_term - cross).reshape(block_shape)
        field_term = field_term + coupled[..., 0:1] * left_block + coupled[..., 1:2] * right_block
        sample = apply_blocks(block_cov, field_term.reshape(local_f, -1, block_width)) + noise_draw
        chosen = (colours == phase_index)[None, :, None, None]
        current = jnp.where(chosen, sample.reshape(block_shape), blocks).reshape(local_f, sites_dev)
    return current


def solution(mesh):
    placed = (
        P("factor", "region"),
        P(),
        P(),
        P("factor", "region", None),
        P("factor", "region", None, None),
        P("factor", "region", None, None),
        P("factor", "region"),
        P("factor", "region"),
        P("region"),
        P("region", None),
    )
    return jax.shard_map(
        on_device, mesh=mesh, in_specs=placed, out_specs=P("factor", "region"), check_vma=False
    )
```

profile of v0, /device:TPU:1, one launch (start us, length us, event | category | flops | bytes accessed | tf_op | source)
XLA Modules:
  0.0 425.0 jit_solution(11497592514453893577)
XLA Ops:
  6.5 0.0 all-reduce.3.cloned.1.call-start
  6.6 0.7 convert_multiply_fusion
  7.3 0.8 broadcast_multiply_fusion
  8.2 3.6 fusion.27
  11.8 0.0 all-reduce.3.cloned.1.call-update
  11.8 0.2 slice_reduce_fusion.1
  12.1 41.5 %all-gather = f32[8,1,8192]{2,1,0:T(1,128)S(1)} all-gather(f32[1,1,8192]{2,1,0:T(1,128)S(1)} %bitcast.229), channel_id=1, replica_groups=mesh['region'=32,'factor'=8] {'factor'}, dimensions={0}, use_global_device_ids=true | all-gather | bytes 294912 | tf_op jit(solution)/shard_map/all_gather | solution.py:78
  53.6 49.7 %all_gather.25 = f32[1,64,2,128]{3,2,0,1:T(2,128)S(1)} all-gather(f32[1,2,2,128]{3,2,0,1:T(2,128)S(1)} %maximum_bitcast_fusion), channel_id=1, replica_groups=mesh['region'=32,'factor'=8] {'region'}, dimensions={1}, use_global_device_ids=true | all-gather | bytes 67584 | tf_op jit(solution)/shard_map/all_gather | solution.py:80
  103.3 0.1 fusion.36
  103.3 0.1 reshape.378
  103.4 0.6 gather_fusion
  104.0 0.1 bitcast_select_fusion.7
  104.1 0.6 gather_fusion.1
  104.6 0.1 bitcast_select_fusion.6
  104.7 8.3 %fusion = f32[64,1,128]{2,1,0:T(1,128)S(1)} fusion(f32[1,64,128,128]{3,2,1,0:T(8,128)} %param.17, f32[1,8192]{1,0:T(1,128)S(1)} %copy-done), kind=kOutput, calls=%fused_computation.12 | convolution fusion | flops 12582912 | bytes 4259840 | tf_op jit(solution)/shard_map/...ij,...j->...i/dot_general | solution.py:16
  113.0 0.1 mul.114
  113.1 0.1 mul.117
  113.2 0.1 broadcast_in_dim.65
  113.3 0.1 broadcast_in_dim.63
  113.4 0.1 broadcast_in_dim.61
  113.5 0.1 broadcast_in_dim.59
  113.6 0.6 dynamic-slice
  114.2 0.2 convolution_multiply_fusion
  114.4 4.0 all-reduce.3.cloned.1.call-done
  118.5 2.1 convolution_subtract_fusion.3
  120.5 0.1 fusion.25
  120.6 8.3 %fusion.8 = f32[64,1,128]{2,1,0:T(1,128)S(1)} fusion(f32[64,128,1]{1,2,0:T(1,128)S(1)} %bitcast.249, f32[1,64,128,128]{3,2,1,0:T(8,128)} %param.16), kind=kOutput, calls=%fused_computation.20 | convolution fusion | flops 12582912 | bytes 4259840 | tf_op jit(solution)/shard_map/...ij,...j->...i/dot_general | solution.py:16
  128.9 0.1 broadcast_select_fusion.2
  129.1 46.8 %all_gather.27 = f32[1,64,2,128]{3,2,0,1:T(2,128)S(1)} all-gather(f32[1,2,2,128]{3,2,0,1:T(2,128)S(1)} %maximum_bitcast_fusion.1), channel_id=1, replica_groups=mesh['region'=32,'factor'=8] {'region'}, dimensions={1}, use_global_device_ids=true | all-gather | bytes 67584 | tf_op jit(solution)/shard_map/all_gather | solution.py:80
  175.9 0.1 fusion.35
  176.0 0.6 gather_fusion.2
  176.5 0.1 bitcast_select_fusion.5
  176.6 0.6 gather_fusion.3
  177.1 0.1 bitcast_select_fusion.4
  177.2 0.1 select_n.93
  177.3 38.3 %all-gather.1 = f32[8,1,8192]{2,1,0:T(1,128)S(1)} all-gather(f32[1,1,8192]{2,1,0:T(1,128)S(1)} %bitcast.242), channel_id=1, replica_groups=mesh['region'=32,'factor'=8] {'factor'}, dimensions={0}, use_global_device_ids=true | all-gather | bytes 294912 | tf_op jit(solution)/shard_map/all_gather | solution.py:78
  215.6 2.1 convolution_subtract_fusion.2
  217.7 0.1 fusion.23
  217.8 8.3 %fusion.6 = f32[64,1,128]{2,1,0:T(1,128)S(1)} fusion(f32[64,128,1]{1,2,0:T(1,128)S(1)} %bitcast.250, f32[1,64,128,128]{3,2,1,0:T(8,128)} %param.16), kind=kOutput, calls=%fused_computation.18 | convolution fusion | flops 12582912 | bytes 4259840 | tf_op jit(solution)/shard_map/...ij,...j->...i/dot_general | solution.py:16
  226.1 0.1 broadcast_select_fusion.1
  226.2 44.2 %all_gather.29 = f32[1,64,2,128]{3,2,0,1:T(2,128)S(1)} all-gather(f32[1,2,2,128]{3,2,0,1:T(2,128)S(1)} %maximum_bitcast_fusion.2), channel_id=1, replica_groups=mesh['region'=32,'factor'=8] {'region'}, dimensions={1}, use_global_device_ids=true | all-gather | bytes 67584 | tf_op jit(solution)/shard_map/all_gather | solution.py:80
  270.4 0.1 fusion.34
  270.5 0.6 gather_fusion.4
  271.0 0.1 bitcast_select_fusion.3
  271.1 0.1 select_n.95
  271.2 38.7 %all-gather.2 = f32[8,1,8192]{2,1,0:T(1,128)S(1)} all-gather(f32[1,1,8192]{2,1,0:T(1,128)S(1)} %bitcast.241), channel_id=1, replica_groups=mesh['region'=32,'factor'=8] {'factor'}, dimensions={0}, use_global_device_ids=true | all-gather | bytes 294912 | tf_op jit(solution)/shard_map/all_gather | solution.py:78
  309.9 0.6 gather_fusion.5
  310.4 0.1 bitcast_select_fusion.2
  310.5 2.1 convolution_subtract_fusion.1
  312.6 0.1 fusion.21
  312.7 8.3 %fusion.4 = f32[64,1,128]{2,1,0:T(1,128)S(1)} fusion(f32[64,128,1]{1,2,0:T(1,128)S(1)} %bitcast.251, f32[1,64,128,128]{3,2,1,0:T(8,128)} %param.16), kind=kOutput, calls=%fused_computation.16 | convolution fusion | flops 12582912 | bytes 4259840 | tf_op jit(solution)/shard_map/...ij,...j->...i/dot_general | solution.py:16
  321.0 0.1 broadcast_select_fusion
  321.1 46.1 %all_gather.31 = f32[1,64,2,128]{3,2,0,1:T(2,128)S(1)} all-gather(f32[1,2,2,128]{3,2,0,1:T(2,128)S(1)} %maximum_bitcast_fusion.3), channel_id=1, replica_groups=mesh['region'=32,'factor'=8] {'region'}, dimensions={1}, use_global_device_ids=true | all-gather | bytes 67584 | tf_op jit(solution)/shard_map/all_gather | solution.py:80
  367.2 0.1 fusion.33
  367.3 0.6 gather_fusion.6
  367.9 0.1 bitcast_select_fusion.1
  367.9 0.1 select_n.97
  368.0 38.3 %all-gather.3 = f32[8,1,8192]{2,1,0:T(1,128)S(1)} all-gather(f32[1,1,8192]{2,1,0:T(1,128)S(1)} %bitcast.243), channel_id=1, replica_groups=mesh['region'=32,'factor'=8] {'factor'}, dimensions={0}, use_global_device_ids=true | all-gather | bytes 294912 | tf_op jit(solution)/shard_map/all_gather | solution.py:78
  406.3 0.6 gather_fusion.7
  406.9 0.1 bitcast_select_fusion
  407.0 2.1 convolution_subtract_fusion
  409.1 0.1 fusion.19
  409.2 8.3 %fusion.2 = f32[64,1,128]{2,1,0:T(1,128)S(1)} fusion(f32[64,128,1]{1,2,0:T(1,128)S(1)} %bitcast.248, f32[1,64,128,128]{3,2,1,0:T(8,128)} %param.16), kind=kOutput, calls=%fused_computation.14 | convolution fusion | flops 12582912 | bytes 4259840 | tf_op jit(solution)/shard_map/...ij,...j->...i/dot_general | solution.py:16
  417.5 0.7 select_n.99
  (48 shorter events, 0.4 us)
Async XLA Ops:
  6.5 98.2 %copy-start = (f32[1,8192]{1,0:T(1,128)S(1)}, f32[1,8192]{1,0:T(1,128)}, u32[]{:S(2)}) copy-start(f32[1,8192]{1,0:T(1,128)} %param.18) | copy-start | bytes 98308
  6.5 5.3 %copy-start.3 = (s32[2,2]{1,0:T(2,128)S(1)}, s32[2,2]{1,0:T(2,128)}, u32[]{:S(2)}) copy-start(s32[2,2]{1,0:T(2,128)} %param.21) | copy-start | bytes 52
  6.5 5.5 %copy-start.1 = (f32[1,8192]{1,0:T(1,128)S(1)}, f32[1,8192]{1,0:T(1,128)}, u32[]{:S(2)}) copy-start(f32[1,8192]{1,0:T(1,128)} %param.19) | copy-start | bytes 98308
  6.5 96.8 %copy-start.4 = (f32[1,64,2]{1,2,0:T(2,128)S(1)}, f32[1,64,2]{1,2,0:T(2,128)}, u32[]{:S(2)}) copy-start(f32[1,64,2]{1,2,0:T(2,128)} %param.15) | copy-start | bytes 1540
  6.5 96.9 %copy-start.5 = (s32[2]{0:T(128)S(1)}, s32[2]{0:T(128)}, u32[]{:S(2)}) copy-start(s32[2]{0:T(128)} %param.20) | copy-start | bytes 28
  6.5 111.9 %all-reduce.3.cloned.1.call-start = ((), (), s32[]{:S(2)}) async-start(), calls=%async_computation | async-start | bytes 524288
  8.2 105.5 %copy-start.6 = (u32[256]{0:T(256)S(1)}, u32[256]{0:T(256)}, u32[]{:S(2)}) copy-start(u32[256]{0:T(256)} %constant.43) | copy-start | bytes 3076
  8.2 106.1 %copy-start.2 = (f32[2000,8]{0,1:T(8,128)S(1)}, f32[2000,8]{0,1:T(8,128)}, u32[]{:S(2)}) copy-start(f32[2000,8]{0,1:T(8,128)} %param.13) | copy-start | bytes 192004
Sparse Core Ops, SparseCore 0:
  11.9 106.4 all-reduce.2
where the time goes:
time: 429 us; the launch traced here: 425 us
  blocking collectives  344 us (80%)
  matrix products  53.6 us (12%)
  between operations  13.8 us (3%)
  local copies, waits for them, and re-layouts  6.15 us (1%)
    all_gather x4, blocking collectives, on_device(): lax.all_gather(end_stack(current, block_shape), 'region', axis=1, tiled=T...  187 us
    all_gather x4, blocking collectives, on_device(): lax.all_gather(current, 'factor', axis=0, tiled=True)  157 us
    dot_general x5, matrix products, apply_blocks(): jnp.einsum('...ij,...j->...i', matrices, vectors, precision=exact_mode)  41.5 us
  transfers between devices with their start and end apart: 1, of which 1 were waited for; matrix products, arithmetic and copies ran while one was open for 3% of the time, Pallas kernels for 0%

commit v1 on v0

v1 whole, which is shorter than its diff:
```python
import functools
import math

import jax
import jax.numpy as jnp
from jax import lax
from jax.experimental import pallas as pl
from jax.experimental.pallas import tpu as pltpu
from jax.sharding import PartitionSpec as P

MESH = pl.DeviceIdType.MESH
LANES = 128
CHUNKS = (
    ((0, 4), (28, 8), (60, 4)),
    ((4, 16),),
    ((20, 8), (36, 8)),
    ((44, 16),),
)
PER_CHUNK = 16
ENDS = (0, 7, 8, 15)


def kernel(
    species_total,
    resp_hbm,
    load_hbm,
    obs_hbm,
    coup_hbm,
    cov_hbm,
    nf_hbm,
    noise_hbm,
    lat_hbm,
    col_hbm,
    par_hbm,
    out_ref,
    resp_v,
    load_v,
    obs_v,
    coup_v,
    cov_v,
    nf_v,
    noise_v,
    lat_v,
    col_s,
    par_s,
    draw_v,
    local_v,
    field_v,
    c0_v,
    c1_v,
    part_v,
    x_recv,
    z_send,
    z_recv,
    keep_v,
    old_v,
    new_v,
    small_sem,
    resp_sem,
    nf_sem,
    cov_sem,
    x_ssem,
    x_rsem,
    z_ssem,
    z_rsem,
    old_ssem,
    old_rsem,
    new_ssem,
    new_rsem,
):
    n_chunks = len(CHUNKS)
    factors = load_v.shape[0]
    species_local = resp_v.shape[1]
    region_n = lax.axis_size("region")
    ri = lax.axis_index("region")
    fi = lax.axis_index("factor")
    xi = fi // 2
    zi = fi % 2

    small = [
        pltpu.make_async_copy(src, dst, small_sem.at[i])
        for i, (src, dst) in enumerate(
            (
                (load_hbm, load_v),
                (obs_hbm, obs_v),
                (lat_hbm, lat_v),
                (coup_hbm, coup_v),
                (noise_hbm, noise_v),
                (col_hbm, col_s),
                (par_hbm, par_s),
            )
        )
    ]
    for copy in small:
        copy.start()
    resp_in, nf_in, cov_in = [], [], []
    for c, runs in enumerate(CHUNKS):
        at, rows = 0, []
        for i, (first, count) in enumerate(runs):
            rows.append(
                pltpu.make_async_copy(
                    resp_hbm.at[:, pl.ds(first * LANES, count * LANES)],
                    resp_v.at[c, :, pl.ds(at * LANES, count * LANES)],
                    resp_sem.at[c, i],
                )
            )
            at += count
        resp_in.append(rows)
    for hbm, ref, sem, out in ((nf_hbm, nf_v, nf_sem, nf_in), (cov_hbm, cov_v, cov_sem, cov_in)):
        for c, runs in enumerate(CHUNKS):
            at, rows = c * PER_CHUNK, []
            for i, (first, count) in enumerate(runs):
                rows.append(
                    pltpu.make_async_copy(
                        hbm.at[pl.ds(first, count)], ref.at[pl.ds(at, count)], sem.at[c, i]
                    )
                )
                at += count
            out.append(rows)
    for group in (resp_in, nf_in, cov_in):
        for rows in group:
            for copy in rows:
                copy.start()

    x_peers = [lax.rem(xi + d, 4) * 2 + zi for d in (1, 2, 3)]
    z_peer = xi * 2 + (1 - zi)
    barrier = pltpu.get_barrier_semaphore()
    for peer in x_peers + [z_peer]:
        pl.semaphore_signal(barrier, inc=1, device_id={"factor": peer}, device_id_type=MESH)

    @pl.loop(1, region_n)
    def _(d):
        pl.semaphore_signal(
            barrier, inc=1, device_id={"region": lax.rem(ri + d, region_n)}, device_id_type=MESH
        )

    small[0].wait()
    small[1].wait()
    tau = obs_v[...].astype(jnp.float32) * (0.25 / math.sqrt(species_total))
    weighted = load_v[...] * tau
    own_load = load_v[pl.ds(fi, 1), :]
    gram = jnp.sum(weighted * own_load, axis=1, keepdims=True)
    gram = jnp.where(lax.broadcasted_iota(jnp.int32, gram.shape, 0) == fi, 0.0, gram)
    mine = weighted[:, :species_local]
    for k in range(1, factors):
        mine = jnp.where(fi == k, weighted[:, k * species_local : (k + 1) * species_local], mine)
    mine = mine.astype(jnp.bfloat16)
    gram = jnp.broadcast_to(gram, (factors, LANES))

    small[2].wait()
    small[5].wait()
    nb = lat_v.shape[0]
    half = nb // 2
    old_v[ri, pl.ds(0, 1), :] = lat_v[0:1, :]
    old_v[ri, pl.ds(1, 1), :] = lat_v[half - 1 : half, :]
    old_v[ri, pl.ds(2, 1), :] = lat_v[half : half + 1, :]
    old_v[ri, pl.ds(3, 1), :] = lat_v[nb - 1 : nb, :]
    for q in range(2):
        old_v[ri, pl.ds(4 + q, 1), :] = jnp.full((1, LANES), col_s[q].astype(jnp.float32))

    def partial_term(c):
        for copy in resp_in[c]:
            copy.wait()
        term = jnp.dot(mine, resp_v[c], preferred_element_type=jnp.float32)
        at = 0
        for first, count in CHUNKS[c]:
            for k in range(count):
                row = lat_v[first + k : first + k + 1, :]
                value = term[:, at * LANES : (at + 1) * LANES] - gram * row
                part_v[c, pl.ds(at, factors, stride=PER_CHUNK), :] = value
                at += 1

    def x_copies(c):
        copies = []
        for d in range(3):
            start = pl.multiple_of((x_peers[d] - zi) * PER_CHUNK, 2 * PER_CHUNK)
            copies.append(
                pltpu.make_async_remote_copy(
                    src_ref=part_v.at[c, pl.ds(start, 2 * PER_CHUNK)],
                    dst_ref=x_recv.at[c, d],
                    send_sem=x_ssem.at[c, d],
                    recv_sem=x_rsem.at[c, d],
                    device_id={"factor": x_peers[d]},
                    device_id_type=MESH,
                )
            )
        return copies

    def z_copy(c):
        return pltpu.make_async_remote_copy(
            src_ref=z_send.at[c],
            dst_ref=z_recv.at[c],
            send_sem=z_ssem.at[c],
            recv_sem=z_rsem.at[c],
            device_id={"factor": z_peer},
            device_id_type=MESH,
        )

    def send_all(buf, ssem, rsem):
        @pl.loop(1, region_n)
        def _(d):
            pltpu.make_async_remote_copy(
                src_ref=buf.at[ri],
                dst_ref=buf.at[ri],
                send_sem=ssem,
                recv_sem=rsem,
                device_id={"region": lax.rem(ri + d, region_n)},
                device_id_type=MESH,
            ).start()

    def wait_all(buf, sem):
        others = buf.at[pl.ds(0, region_n - 1)]
        pltpu.make_async_copy(others, others, sem).wait()

    partial_term(0)
    pl.semaphore_wait(barrier, 4 + region_n - 1)
    xs = [x_copies(c) for c in range(n_chunks)]
    zs = [z_copy(c) for c in range(n_chunks)]
    for copy in xs[0]:
        copy.start()
    send_all(old_v, old_ssem, old_rsem)
    for c in range(1, n_chunks):
        partial_term(c)
        for copy in xs[c]:
            copy.start()

    diagonal = lax.broadcasted_iota(jnp.int32, (LANES, LANES), 0) == lax.broadcasted_iota(
        jnp.int32, (LANES, LANES), 1
    )

    def times(matrix, row):
        sums = jnp.sum(matrix * row, axis=1, keepdims=True)
        return jnp.sum(jnp.where(diagonal, sums, 0.0), axis=0, keepdims=True)

    small[3].wait()
    pick = lax.broadcasted_iota(jnp.int32, (nb, nb), 0) == lax.broadcasted_iota(
        jnp.int32, (nb, nb), 1
    )
    for i, ref in ((0, c0_v), (1, c1_v)):
        column = jnp.sum(jnp.where(pick, coup_v[i : i + 1, :], 0.0), axis=1, keepdims=True)
        ref[...] = jnp.broadcast_to(column, (nb, LANES))
    rows_at = lax.broadcasted_iota(jnp.int32, (nb, LANES), 0)
    left = pltpu.roll(lat_v[...], 1, 0)
    left = jnp.where((rows_at == 0) | (rows_at == half), 0.0, left)
    right = pltpu.roll(lat_v[...], nb - 1, 0)
    right = jnp.where((rows_at == half - 1) | (rows_at == nb - 1), 0.0, right)
    local_v[...] = c0_v[...] * left + c1_v[...] * right
    small[4].wait()

    def draw(c):
        for copy in nf_in[c]:
            copy.wait()
        at = c * PER_CHUNK
        for first, count in CHUNKS[c]:

            @pl.loop(0, count // 4)
            def _(g, at=at, first=first):
                for k in range(4):
                    row = noise_v[pl.ds(first + 4 * g + k, 1), :]
                    draw_v[pl.ds(first + 4 * g + k, 1), :] = times(nf_v[at + 4 * g + k], row)

            at += count

    def x_sum(c):
        for copy in xs[c]:
            copy.wait_recv()
        at = pl.multiple_of(fi * PER_CHUNK, PER_CHUNK)
        to = pl.multiple_of(z_peer * PER_CHUNK, PER_CHUNK)
        mine_at = pl.multiple_of(zi * PER_CHUNK, PER_CHUNK)
        other_at = pl.multiple_of((1 - zi) * PER_CHUNK, PER_CHUNK)
        out = part_v[c, pl.ds(to, PER_CHUNK), :]
        for d in range(3):
            out = out + x_recv[c, d, pl.ds(other_at, PER_CHUNK), :]
        z_send[c] = out
        zs[c].start()
        own = part_v[c, pl.ds(at, PER_CHUNK), :]
        for d in range(3):
            own = own + x_recv[c, d, pl.ds(mine_at, PER_CHUNK), :]
        keep_v[c] = own

    def z_sum(c):
        zs[c].wait_recv()
        total = keep_v[c] + z_recv[c]
        at = 0
        for first, count in CHUNKS[c]:
            field_v[first : first + count, :] = (
                total[at : at + count, :] + local_v[first : first + count, :]
            )
            at += count

    def blocks(c):
        for copy in cov_in[c]:
            copy.wait()
        at = c * PER_CHUNK
        for first, count in CHUNKS[c]:

            @pl.loop(0, count // 4)
            def _(g, at=at, first=first):
                for k in range(4):
                    b = first + 4 * g + k
                    row = field_v[pl.ds(b, 1), :]
                    out_ref[pl.ds(b, 1), :] = (
                        times(cov_v[at + 4 * g + k], row) + draw_v[pl.ds(b, 1), :]
                    )

            at += count

    def partner_edge(ref, q, side):
        g = par_s[q, side]
        return ref[g // 2, pl.ds(2 * (g % 2) + (1 - side), 1), :]

    def partner_colour(q, side):
        g = par_s[q, side]
        return old_v[g // 2, pl.ds(4 + g % 2, 1), :]

    ends = [
        (q, side, (q * half, q * half + half - 1)[side], ENDS[2 * q + side])
        for q in range(2)
        for side in range(2)
    ]

    draw(0)
    x_sum(0)
    draw(1)
    x_sum(1)
    draw(2)
    z_sum(0)
    small[6].wait()
    for copy in cov_in[0]:
        copy.wait()
    wait_all(old_v, old_rsem)
    for q, side, b, at in ends:
        weight = (c0_v, c1_v)[side][b : b + 1, :]
        row = field_v[b : b + 1, :] + weight * partner_edge(old_v, q, side)
        new_v[ri, pl.ds(2 * q + side, 1), :] = times(cov_v[at], row) + draw_v[b : b + 1, :]
    send_all(new_v, new_ssem, new_rsem)
    x_sum(2)
    draw(3)
    x_sum(3)
    cov_in[0] = []
    for c in range(n_chunks):
        if c:
            z_sum(c)
        blocks(c)
    wait_all(new_v, new_rsem)
    for q, side, b, at in ends:
        weight = (c0_v, c1_v)[side][b : b + 1, :]
        own = jnp.full((1, LANES), col_s[q].astype(jnp.float32))
        edge = jnp.where(
            partner_colour(q, side) < own,
            partner_edge(new_v, q, side),
            partner_edge(old_v, q, side),
        )
        row = field_v[b : b + 1, :] + weight * edge
        out_ref[b : b + 1, :] = times(cov_v[at], row) + draw_v[b : b + 1, :]

    for c in range(n_chunks):
        for copy in xs[c]:
            copy.wait_send()
        zs[c].wait_send()
    wait_all(old_v, old_ssem)
    wait_all(new_v, new_ssem)


def on_device(
    response,
    loadings,
    obs_count,
    couplings,
    block_cov,
    noise_factor,
    noise,
    latents,
    colours,
    partners,
):
    f32 = jnp.float32
    factors = loadings.shape[1]
    species = loadings.shape[0]
    nb = block_cov.shape[1]
    region_n = lax.axis_size("region")
    n_chunks = len(CHUNKS)
    runs = max(len(c) for c in CHUNKS)
    any_spec = pl.BlockSpec(memory_space=pl.ANY)
    dma = pltpu.SemaphoreType.DMA
    out = pl.pallas_call(
        functools.partial(kernel, species),
        out_shape=jax.ShapeDtypeStruct((nb, LANES), f32),
        in_specs=[any_spec] * 10,
        out_specs=pl.BlockSpec(memory_space=pltpu.VMEM),
        scratch_shapes=[
            pltpu.VMEM((n_chunks, response.shape[0], PER_CHUNK * LANES), jnp.bfloat16),
            pltpu.VMEM((factors, species), f32),
            pltpu.VMEM((1, species), jnp.int32),
            pltpu.VMEM((2, nb), f32),
            pltpu.VMEM((nb, LANES, LANES), f32),
            pltpu.VMEM((nb, LANES, LANES), f32),
            pltpu.VMEM((nb, LANES), f32),
            pltpu.VMEM((nb, LANES), f32),
            pltpu.SMEM((2,), jnp.int32),
            pltpu.SMEM((2, 2), jnp.int32),
            pltpu.VMEM((nb, LANES), f32),
            pltpu.VMEM((nb, LANES), f32),
            pltpu.VMEM((nb, LANES), f32),
            pltpu.VMEM((nb, LANES), f32),
            pltpu.VMEM((nb, LANES), f32),
            pltpu.VMEM((n_chunks, factors * PER_CHUNK, LANES), f32),
            pltpu.VMEM((n_chunks, 3, 2 * PER_CHUNK, LANES), f32),
            pltpu.VMEM((n_chunks, PER_CHUNK, LANES), f32),
            pltpu.VMEM((n_chunks, PER_CHUNK, LANES), f32),
            pltpu.VMEM((n_chunks, PER_CHUNK, LANES), f32),
            pltpu.VMEM((region_n, 8, LANES), f32),
            pltpu.VMEM((region_n, 4, LANES), f32),
            dma((7,)),
            dma((n_chunks, runs)),
            dma((n_chunks, runs)),
            dma((n_chunks, runs)),
            dma((n_chunks, 3)),
            dma((n_chunks, 3)),
            dma((n_chunks,)),
            dma((n_chunks,)),
            dma,
            dma,
            dma,
            dma,
        ],
        compiler_params=pltpu.CompilerParams(
            collective_id=0, has_side_effects=True, vmem_limit_bytes=40 * 2**20
        ),
        cost_estimate=pl.CostEstimate(flops=40_000_000, bytes_accessed=13_000_000, transcendentals=0),
        name="sweep",
    )(
        response,
        loadings.T,
        obs_count.reshape(1, species),
        couplings.reshape(nb, 2).T,
        block_cov.reshape(nb, LANES, LANES),
        noise_factor.reshape(nb, LANES, LANES),
        noise.reshape(nb, LANES),
        latents.reshape(nb, LANES),
        colours,
        partners,
    )
    return out.reshape(1, nb * LANES)


def solution(mesh):
    placed = (
        P("factor", "region"),
        P(),
        P(),
        P("factor", "region", None),
        P("factor", "region", None, None),
        P("factor", "region", None, None),
        P("factor", "region"),
        P("factor", "region"),
        P("region"),
        P("region", None),
    )
    return jax.shard_map(
        on_device, mesh=mesh, in_specs=placed, out_specs=P("factor", "region"), check_vma=False
    )
```

time: 429 us -> 39.4 us (0.09)
  blocking collectives: 344 us -> 0 us
  matrix products: 53.6 us -> 0 us
  Pallas kernels: 0 us -> 26.7 us
  between operations: 13.8 us -> 0.02 us
  local copies, waits for them, and re-layouts: 6.15 us -> 12.2 us
    all_gather x8 -> x0, blocking collectives: 344 us -> none  [the longest x4 187 us: on_device(): lax.all_gather(end_stack(current, block_shape), 'region', axis=1, tiled=T...]
    dot_general x11 -> x0, matrix products: 53.6 us -> none  [the longest x5 41.5 us: apply_blocks(): jnp.einsum('...ij,...j->...i', matrices, vectors, precision=exact_mode)]
    pallas_call x0 -> x1, Pallas kernels: none -> 26.7 us  [on_device(): pl.pallas_call(functools.partial(kernel, species), out_shape=jax.ShapeDty...]
    unnamed x15 -> x21, local copies, waits for them, and re-layouts: 0.62 us -> 12.2 us
    gather x8 -> x0, local copies, waits for them, and re-layouts: 4.46 us -> none  [the longest x4 2.23 us: pick_edges(): left_edge = jnp.take(gathered[:, :, 1], partners[:, 0], axis=1)]
  transfers between devices with their start and end apart: 1 -> 0, of which waited for: 1 -> 0; matrix products, arithmetic and copies ran while one was open for 3% -> 0% of each run, Pallas kernels for 0% -> 0%
where the time goes in v1:
time: 39.4 us; the launch traced here: 39 us
  Pallas kernels  26.7 us (68%)
  local copies, waits for them, and re-layouts  12.2 us (31%)
    pallas_call x1, Pallas kernels, on_device(): pl.pallas_call(functools.partial(kernel, species), out_shape=jax.ShapeDty...  26.7 us
    unnamed x21, local copies, waits for them, and re-layouts  12.2 us

profile of v1, /device:TPU:1, one launch (start us, length us, event | category | flops | bytes accessed | tf_op | source)
XLA Modules:
  0.0 39.0 jit_solution(16983777915428222875)
XLA Ops:
  0.0 0.0 copy-start
  0.0 2.2 %copy-done = bf16[250,8192]{1,0:T(8,128)(2,1)S(1)} copy-done((bf16[250,8192]{1,0:T(8,128)(2,1)S(1)}, bf16[250,8192]{1,0:T(8,128)(2,1)}, u32[]{:S(2)}) %copy-start) | copy-done | bytes 4096024
  2.2 0.0 copy-start.1
  2.2 2.2 %copy-done.1 = f32[1,64,128,128]{3,2,1,0:T(8,128)S(1)} copy-done((f32[1,64,128,128]{3,2,1,0:T(8,128)S(1)}, f32[1,64,128,128]{3,2,1,0:T(8,128)}, u32[]{:S(2)}) %copy-start.1) | copy-done | bytes 4194328
  4.4 0.0 copy-start.2
  4.4 2.2 %copy-done.2 = f32[1,64,128,128]{3,2,1,0:T(8,128)S(1)} copy-done((f32[1,64,128,128]{3,2,1,0:T(8,128)S(1)}, f32[1,64,128,128]{3,2,1,0:T(8,128)}, u32[]{:S(2)}) %copy-start.2) | copy-done | bytes 4194328
  6.6 0.0 copy-start.3
  6.6 0.8 %copy-done.3 = f32[2000,8]{0,1:T(8,128)S(1)} copy-done((f32[2000,8]{0,1:T(8,128)S(1)}, f32[2000,8]{0,1:T(8,128)}, u32[]{:S(2)}) %copy-start.3) | copy-done | bytes 64024
  7.4 0.0 copy-start.4
  7.4 0.8 %copy-done.4 = f32[1,8192]{1,0:T(1,128)S(1)} copy-done((f32[1,8192]{1,0:T(1,128)S(1)}, f32[1,8192]{1,0:T(1,128)}, u32[]{:S(2)}) %copy-start.4) | copy-done | bytes 32792
  8.2 0.0 copy-start.5
  8.2 0.8 %copy-done.5 = f32[1,8192]{1,0:T(1,128)S(1)} copy-done((f32[1,8192]{1,0:T(1,128)S(1)}, f32[1,8192]{1,0:T(1,128)}, u32[]{:S(2)}) %copy-start.5) | copy-done | bytes 32792
  8.9 0.0 copy-start.6
  8.9 0.7 %copy-done.6 = s32[2000]{0:T(1024)S(1)} copy-done((s32[2000]{0:T(1024)S(1)}, s32[2000]{0:T(1024)}, u32[]{:S(2)}) %copy-start.6) | copy-done | bytes 8024
  9.6 0.0 copy-start.7
  9.6 0.7 %copy-done.7 = f32[1,64,2]{1,2,0:T(2,128)S(1)} copy-done((f32[1,64,2]{1,2,0:T(2,128)S(1)}, f32[1,64,2]{1,2,0:T(2,128)}, u32[]{:S(2)}) %copy-start.7) | copy-done | bytes 536
  10.3 0.0 copy-start.8
  10.3 0.7 %copy-done.8 = s32[2,2]{1,0:T(2,128)S(1)} copy-done((s32[2,2]{1,0:T(2,128)S(1)}, s32[2,2]{1,0:T(2,128)}, u32[]{:S(2)}) %copy-start.8) | copy-done | bytes 40
  11.0 0.0 copy-start.9
  11.0 0.7 %copy-done.9 = s32[2]{0:T(128)S(1)} copy-done((s32[2]{0:T(128)S(1)}, s32[2]{0:T(128)}, u32[]{:S(2)}) %copy-start.9) | copy-done | bytes 32
  11.6 26.7 %sweep.1 = f32[64,128]{1,0:T(8,128)S(1)} custom-call(bf16[250,8192]{1,0:T(8,128)(2,1)S(1)} %copy-done, f32[8,2000]{1,0:T(8,128)S(1)} %bitcast.13, s32[1,2000]{1,0:T(1,128)S(1)} %bitcast.16, f32[2,64]{1,0:T(2,128)S(1)} %bitcast.17, f32[64,128,128]{2,1,0:T(8,128)S(1)} %bitcast.10, f32[64,128,128]{2,1,0:T(8,128)S(1)} %bitcast.11, f32[64,128]{1,0:T(8,128)S(1)} %bitcast.14, ...), custom_call_target="tpu_custom_call" | custom-call | flops 40000000 | bytes 13000000 | tf_op jit(solution)/shard_map/sweep/pallas_call | solution.py:386
  38.3 0.6 %copy.12 = f32[1,8192]{1,0:T(1,128)} copy(f32[1,8192]{1,0:T(1,128)S(1)} %bitcast.12) | data formatting | bytes 65536
Async XLA Ops:
  0.0 2.2 %copy-start = (bf16[250,8192]{1,0:T(8,128)(2,1)S(1)}, bf16[250,8192]{1,0:T(8,128)(2,1)}, u32[]{:S(2)}) copy-start(bf16[250,8192]{1,0:T(8,128)(2,1)} %resp_hbm.1) | copy-start | bytes 12288004
  2.2 2.2 %copy-start.1 = (f32[1,64,128,128]{3,2,1,0:T(8,128)S(1)}, f32[1,64,128,128]{3,2,1,0:T(8,128)}, u32[]{:S(2)}) copy-start(f32[1,64,128,128]{3,2,1,0:T(8,128)} %param.14) | copy-start | bytes 12582916
  4.4 2.2 %copy-start.2 = (f32[1,64,128,128]{3,2,1,0:T(8,128)S(1)}, f32[1,64,128,128]{3,2,1,0:T(8,128)}, u32[]{:S(2)}) copy-start(f32[1,64,128,128]{3,2,1,0:T(8,128)} %param.15) | copy-start | bytes 12582916
  6.6 0.8 %copy-start.3 = (f32[2000,8]{0,1:T(8,128)S(1)}, f32[2000,8]{0,1:T(8,128)}, u32[]{:S(2)}) copy-start(f32[2000,8]{0,1:T(8,128)} %param.11) | copy-start | bytes 192004
  7.4 0.8 %copy-start.4 = (f32[1,8192]{1,0:T(1,128)S(1)}, f32[1,8192]{1,0:T(1,128)}, u32[]{:S(2)}) copy-start(f32[1,8192]{1,0:T(1,128)} %param.16) | copy-start | bytes 98308
  8.2 0.8 %copy-start.5 = (f32[1,8192]{1,0:T(1,128)S(1)}, f32[1,8192]{1,0:T(1,128)}, u32[]{:S(2)}) copy-start(f32[1,8192]{1,0:T(1,128)} %param.17) | copy-start | bytes 98308
  8.9 0.7 %copy-start.6 = (s32[2000]{0:T(1024)S(1)}, s32[2000]{0:T(1024)}, u32[]{:S(2)}) copy-start(s32[2000]{0:T(1024)} %param.12) | copy-start | bytes 24004
  9.6 0.7 %copy-start.7 = (f32[1,64,2]{1,2,0:T(2,128)S(1)}, f32[1,64,2]{1,2,0:T(2,128)}, u32[]{:S(2)}) copy-start(f32[1,64,2]{1,2,0:T(2,128)} %param.13) | copy-start | bytes 1540
  10.3 0.7 %copy-start.8 = (s32[2,2]{1,0:T(2,128)S(1)}, s32[2,2]{1,0:T(2,128)}, u32[]{:S(2)}) copy-start(s32[2,2]{1,0:T(2,128)} %par_hbm.1) | copy-start | bytes 52
  11.0 0.7 %copy-start.9 = (s32[2]{0:T(128)S(1)}, s32[2]{0:T(128)}, u32[]{:S(2)}) copy-start(s32[2]{0:T(128)} %col_hbm.1) | copy-start | bytes 28

commit v2 on v1

--- a/solution.py
+++ b/solution.py
@@ -381,7 +381,7 @@
     region_n = lax.axis_size("region")
     n_chunks = len(CHUNKS)
     runs = max(len(c) for c in CHUNKS)
-    any_spec = pl.BlockSpec(memory_space=pl.ANY)
+    any_spec = pl.BlockSpec(memory_space=pltpu.HBM)
     dma = pltpu.SemaphoreType.DMA
     out = pl.pallas_call(
         functools.partial(kernel, species),
@@ -425,7 +425,7 @@
             dma,
         ],
         compiler_params=pltpu.CompilerParams(
-            collective_id=0, has_side_effects=True, vmem_limit_bytes=40 * 2**20
+            collective_id=0, has_side_effects=True, vmem_limit_bytes=60 * 2**20
         ),
         cost_estimate=pl.CostEstimate(flops=40_000_000, bytes_accessed=13_000_000, transcendentals=0),
         name="sweep",

time: 39.4 us -> 27.8 us (0.71)
  local copies, waits for them, and re-layouts: 12.2 us -> 1.38 us
  Pallas kernels: 26.7 us -> 26.3 us
    unnamed x21 -> x1, local copies, waits for them, and re-layouts: 12.2 us -> 1.38 us
where the time goes in v2:
time: 27.8 us; the launch traced here: 27.7 us
  Pallas kernels  26.3 us (95%)
  local copies, waits for them, and re-layouts  1.38 us (5%)
    pallas_call x1, Pallas kernels, on_device(): pl.pallas_call(functools.partial(kernel, species), out_shape=jax.ShapeDty...  26.3 us
    unnamed x1, local copies, waits for them, and re-layouts  1.38 us

profile of v2, /device:TPU:1, one launch (start us, length us, event | category | flops | bytes accessed | tf_op | source)
XLA Modules:
  0.0 27.7 jit_solution(11923515189727585622)
XLA Ops:
  0.0 26.3 %sweep.1 = f32[64,128]{1,0:T(8,128)} custom-call(bf16[250,8192]{1,0:T(8,128)(2,1)} %resp_hbm.1, f32[8,2000]{1,0:T(8,128)} %bitcast.13, s32[1,2000]{1,0:T(1,128)} %bitcast.16, f32[2,64]{1,0:T(2,128)} %bitcast.17, f32[64,128,128]{2,1,0:T(8,128)} %bitcast.10, f32[64,128,128]{2,1,0:T(8,128)} %bitcast.11, f32[64,128]{1,0:T(8,128)} %bitcast.14, ...), custom_call_target="tpu_custom_call" | custom-call | flops 40000000 | bytes 13000000 | tf_op jit(solution)/shard_map/sweep/pallas_call | solution.py:386
  26.3 1.4 %copy.12 = f32[1,8192]{1,0:T(1,128)} copy(f32[1,8192]{1,0:T(1,128)} %bitcast.12) | data formatting | bytes 65536

commit v3 on v2

v3 whole, which is shorter than its diff:
```python
import functools
import math

import jax
import jax.numpy as jnp
from jax import lax
from jax.experimental import pallas as pl
from jax.experimental.pallas import tpu as pltpu
from jax.sharding import PartitionSpec as P

MESH = pl.DeviceIdType.MESH
LANES = 128
CHUNKS = 4


def kernel(
    species_total,
    resp_hbm,
    load_hbm,
    obs_hbm,
    coup_hbm,
    cov_hbm,
    nf_hbm,
    noise_hbm,
    lat_hbm,
    col_hbm,
    par_hbm,
    out_ref,
    resp_v,
    rend_v,
    load_v,
    obs_v,
    coup_v,
    cov_v,
    nf_v,
    noise_v,
    lat_v,
    col_s,
    par_s,
    draw_v,
    local_v,
    field_v,
    c0_v,
    c1_v,
    part_v,
    x_recv,
    y_recv,
    z_send,
    z_recv,
    end_v,
    end_recv,
    old_v,
    new_v,
    small_sem,
    rend_sem,
    resp_sem,
    nf_sem,
    cov_sem,
    x_ssem,
    x_rsem,
    y_ssem,
    y_rsem,
    z_ssem,
    z_rsem,
    end_ssem,
    end_rsem,
    old_ssem,
    old_rsem,
    new_ssem,
    new_rsem,
):
    factors = load_v.shape[0]
    species_local = resp_v.shape[1]
    nb = lat_v.shape[0]
    half = nb // 2
    per = nb // CHUNKS
    region_n = lax.axis_size("region")
    ri = lax.axis_index("region")
    fi = lax.axis_index("factor")
    xi = fi // 2
    zi = fi % 2
    end_blocks = (0, half - 1, half, nb - 1)

    small = [
        pltpu.make_async_copy(src, dst, small_sem.at[i])
        for i, (src, dst) in enumerate(
            (
                (load_hbm, load_v),
                (obs_hbm, obs_v),
                (lat_hbm, lat_v),
                (coup_hbm, coup_v),
                (noise_hbm, noise_v),
                (col_hbm, col_s),
                (par_hbm, par_s),
            )
        )
    ]
    rend_in = [
        pltpu.make_async_copy(
            resp_hbm.at[:, pl.ds(b * LANES, LANES)],
            rend_v.at[:, pl.ds(i * LANES, LANES)],
            rend_sem.at[i],
        )
        for i, b in enumerate(end_blocks)
    ]
    resp_in = [
        pltpu.make_async_copy(
            resp_hbm.at[:, pl.ds(c * per * LANES, per * LANES)], resp_v.at[c], resp_sem.at[c]
        )
        for c in range(CHUNKS)
    ]
    nf_in, cov_in = (
        [
            pltpu.make_async_copy(
                hbm.at[pl.ds(c * per, per)], ref.at[pl.ds(c * per, per)], sem.at[c]
            )
            for c in range(CHUNKS)
        ]
        for hbm, ref, sem in ((nf_hbm, nf_v, nf_sem), (cov_hbm, cov_v, cov_sem))
    )
    for copy in small[:3] + small[5:6] + rend_in + resp_in:
        copy.start()

    x_peers = [lax.rem(xi + d, 4) * 2 for d in (1, 2, 3)]
    z_peer = xi * 2 + (1 - zi)
    barrier = pltpu.get_barrier_semaphore()
    for d in range(1, factors):
        pl.semaphore_signal(
            barrier, inc=1, device_id={"factor": lax.rem(fi + d, factors)}, device_id_type=MESH
        )

    @pl.loop(1, region_n)
    def _(d):
        pl.semaphore_signal(
            barrier, inc=1, device_id={"region": lax.rem(ri + d, region_n)}, device_id_type=MESH
        )

    for copy in small[3:5] + small[6:]:
        copy.start()

    small[0].wait()
    small[1].wait()
    tau = obs_v[...].astype(jnp.float32) * (0.25 / math.sqrt(species_total))
    weighted = load_v[...] * tau
    own_load = load_v[pl.ds(fi, 1), :]
    gram = jnp.sum(weighted * own_load, axis=1, keepdims=True)
    gram = jnp.where(lax.broadcasted_iota(jnp.int32, gram.shape, 0) == fi, 0.0, gram)
    mine = weighted[:, :species_local]
    for k in range(1, factors):
        mine = jnp.where(fi == k, weighted[:, k * species_local : (k + 1) * species_local], mine)
    mine = mine.astype(jnp.bfloat16)
    gram = jnp.broadcast_to(gram, (factors, LANES))

    small[2].wait()
    small[5].wait()
    for i, b in enumerate(end_blocks):
        old_v[ri, pl.ds(i, 1), :] = lat_v[b : b + 1, :]
    for q in range(2):
        old_v[ri, pl.ds(4 + q, 1), :] = jnp.full((1, LANES), col_s[q].astype(jnp.float32))

    for copy in rend_in:
        copy.wait()
    term = jnp.dot(mine, rend_v[...], preferred_element_type=jnp.float32)
    for i, b in enumerate(end_blocks):
        value = term[:, i * LANES : (i + 1) * LANES] - gram * lat_v[b : b + 1, :]
        end_v[pl.ds(i, factors, stride=8), :] = value

    def send_all(buf, ssem, rsem):
        @pl.loop(1, region_n)
        def _(d):
            pltpu.make_async_remote_copy(
                src_ref=buf.at[ri],
                dst_ref=buf.at[ri],
                send_sem=ssem,
                recv_sem=rsem,
                device_id={"region": lax.rem(ri + d, region_n)},
                device_id_type=MESH,
            ).start()

    def wait_all(buf, sem):
        others = buf.at[pl.ds(0, region_n - 1)]
        pltpu.make_async_copy(others, others, sem).wait()

    pl.semaphore_wait(barrier, factors - 1 + region_n - 1)
    ends_out = []
    for d in range(1, factors):
        peer = lax.rem(fi + d, factors)
        ends_out.append(
            pltpu.make_async_remote_copy(
                src_ref=end_v.at[pl.ds(pl.multiple_of(peer * 8, 8), 8)],
                dst_ref=end_recv.at[d - 1],
                send_sem=end_ssem.at[d - 1],
                recv_sem=end_rsem.at[d - 1],
                device_id={"factor": peer},
                device_id_type=MESH,
            )
        )
    for copy in ends_out:
        copy.start()
    send_all(old_v, old_ssem, old_rsem)

    def rows_of(factor, c):
        return pl.ds(pl.multiple_of(factor * nb + c * per, per), per)

    def x_copies(c):
        return [
            pltpu.make_async_remote_copy(
                src_ref=part_v.at[rows_of(x_peers[d] + 1 - zi, c)],
                dst_ref=x_recv.at[c, d],
                send_sem=x_ssem.at[c, d],
                recv_sem=x_rsem.at[c, d],
                device_id={"factor": x_peers[d] + zi},
                device_id_type=MESH,
            )
            for d in range(3)
        ]

    xs = [x_copies(c) for c in range(CHUNKS)]
    ys = [
        pltpu.make_async_remote_copy(
            src_ref=part_v.at[pl.ds(pl.multiple_of((x_peers[d] + zi) * nb, nb), nb)],
            dst_ref=y_recv.at[d],
            send_sem=y_ssem.at[d],
            recv_sem=y_rsem.at[d],
            device_id={"factor": x_peers[d] + zi},
            device_id_type=MESH,
        )
        for d in range(3)
    ]
    zs = [
        pltpu.make_async_remote_copy(
            src_ref=z_send.at[c],
            dst_ref=z_recv.at[c],
            send_sem=z_ssem.at[c],
            recv_sem=z_rsem.at[c],
            device_id={"factor": z_peer},
            device_id_type=MESH,
        )
        for c in range(CHUNKS)
    ]
    for c in range(CHUNKS):
        resp_in[c].wait()
        nf_in[c].start()
        term = jnp.dot(mine, resp_v[c], preferred_element_type=jnp.float32)
        for i in range(per):
            b = c * per + i
            value = term[:, i * LANES : (i + 1) * LANES] - gram * lat_v[b : b + 1, :]
            part_v[pl.ds(b, factors, stride=nb), :] = value
        for copy in xs[c]:
            copy.start()
    for copy in ys:
        copy.start()

    diagonal = lax.broadcasted_iota(jnp.int32, (LANES, LANES), 0) == lax.broadcasted_iota(
        jnp.int32, (LANES, LANES), 1
    )

    def times(matrix, row):
        sums = jnp.sum(matrix * row, axis=1, keepdims=True)
        return jnp.sum(jnp.where(diagonal, sums, 0.0), axis=0, keepdims=True)

    small[3].wait()
    pick = lax.broadcasted_iota(jnp.int32, (nb, nb), 0) == lax.broadcasted_iota(
        jnp.int32, (nb, nb), 1
    )
    for i, ref in ((0, c0_v), (1, c1_v)):
        column = jnp.sum(jnp.where(pick, coup_v[i : i + 1, :], 0.0), axis=1, keepdims=True)
        ref[...] = jnp.broadcast_to(column, (nb, LANES))
    rows_at = lax.broadcasted_iota(jnp.int32, (nb, LANES), 0)
    left = pltpu.roll(lat_v[...], 1, 0)
    left = jnp.where((rows_at == 0) | (rows_at == half), 0.0, left)
    right = pltpu.roll(lat_v[...], nb - 1, 0)
    right = jnp.where((rows_at == half - 1) | (rows_at == nb - 1), 0.0, right)
    local_v[...] = c0_v[...] * left + c1_v[...] * right
    small[4].wait()

    UNROLL = 8

    def draw(c):
        nf_in[c].wait()
        cov_in[c].start()

        @pl.loop(0, per // UNROLL)
        def _(g):
            for k in range(UNROLL):
                b = c * per + UNROLL * g + k
                draw_v[pl.ds(b, 1), :] = times(nf_v[b], noise_v[pl.ds(b, 1), :])

    def x_sum(c):
        for copy in xs[c]:
            copy.wait_recv()
        out = part_v[rows_of(z_peer, c), :]
        for d in range(3):
            out = out + x_recv[c, d]
        z_send[c] = out
        zs[c].start()

    def z_sum(c):
        zs[c].wait_recv()
        here = pl.ds(c * per, per)
        total = part_v[rows_of(fi, c), :] + local_v[here, :] + z_recv[c]
        for d in range(3):
            total = total + y_recv[d, here, :]
        field_v[here, :] = total

    def blocks(c):
        @pl.loop(0, per // UNROLL)
        def _(g):
            for k in range(UNROLL):
                b = c * per + UNROLL * g + k
                row = field_v[pl.ds(b, 1), :]
                out_ref[pl.ds(b, 1), :] = times(cov_v[b], row) + draw_v[pl.ds(b, 1), :]

    def partner_edge(ref, q, side):
        g = par_s[q, side]
        return ref[g // 2, pl.ds(2 * (g % 2) + (1 - side), 1), :]

    def partner_colour(q, side):
        g = par_s[q, side]
        return old_v[g // 2, pl.ds(4 + g % 2, 1), :]

    draw(0)
    draw(1)
    draw(2)
    for c in range(CHUNKS):
        x_sum(c)
    draw(3)

    for copy in ends_out:
        copy.wait_recv()
    own_end = end_v[pl.ds(pl.multiple_of(fi * 8, 8), 8), :]
    for d in range(factors - 1):
        own_end = own_end + end_recv[d]
    small[6].wait()
    for c in range(CHUNKS):
        cov_in[c].wait()
    wait_all(old_v, old_rsem)
    bases = []
    for i, b in enumerate(end_blocks):
        q, side = i // 2, i % 2
        bases.append(own_end[i : i + 1, :] + local_v[b : b + 1, :])
        weight = (c0_v, c1_v)[side][b : b + 1, :]
        row = bases[i] + weight * partner_edge(old_v, q, side)
        new_v[ri, pl.ds(i, 1), :] = times(cov_v[b], row) + draw_v[b : b + 1, :]
    send_all(new_v, new_ssem, new_rsem)

    for copy in ys:
        copy.wait_recv()
    for c in range(CHUNKS):
        z_sum(c)
        blocks(c)
    wait_all(new_v, new_rsem)
    for i, b in enumerate(end_blocks):
        q, side = i // 2, i % 2
        weight = (c0_v, c1_v)[side][b : b + 1, :]
        own = jnp.full((1, LANES), col_s[q].astype(jnp.float32))
        edge = jnp.where(
            partner_colour(q, side) < own,
            partner_edge(new_v, q, side),
            partner_edge(old_v, q, side),
        )
        row = bases[i] + weight * edge
        out_ref[b : b + 1, :] = times(cov_v[b], row) + draw_v[b : b + 1, :]

    for copy in ends_out + ys + zs + [copy for c in range(CHUNKS) for copy in xs[c]]:
        copy.wait_send()
    wait_all(old_v, old_ssem)
    wait_all(new_v, new_ssem)


def on_device(
    response,
    loadings,
    obs_count,
    couplings,
    block_cov,
    noise_factor,
    noise,
    latents,
    colours,
    partners,
):
    f32 = jnp.float32
    factors = loadings.shape[1]
    species = loadings.shape[0]
    nb = block_cov.shape[1]
    region_n = lax.axis_size("region")
    per = nb // CHUNKS
    any_spec = pl.BlockSpec(memory_space=pltpu.HBM)
    dma = pltpu.SemaphoreType.DMA
    out = pl.pallas_call(
        functools.partial(kernel, species),
        out_shape=jax.ShapeDtypeStruct((nb, LANES), f32),
        in_specs=[any_spec] * 10,
        out_specs=pl.BlockSpec(memory_space=pltpu.VMEM),
        scratch_shapes=[
            pltpu.VMEM((CHUNKS, response.shape[0], per * LANES), jnp.bfloat16),
            pltpu.VMEM((response.shape[0], 4 * LANES), jnp.bfloat16),
            pltpu.VMEM((factors, species), f32),
            pltpu.VMEM((1, species), jnp.int32),
            pltpu.VMEM((2, nb), f32),
            pltpu.VMEM((nb, LANES, LANES), f32),
            pltpu.VMEM((nb, LANES, LANES), f32),
            pltpu.VMEM((nb, LANES), f32),
            pltpu.VMEM((nb, LANES), f32),
            pltpu.SMEM((2,), jnp.int32),
            pltpu.SMEM((2, 2), jnp.int32),
            pltpu.VMEM((nb, LANES), f32),
            pltpu.VMEM((nb, LANES), f32),
            pltpu.VMEM((nb, LANES), f32),
            pltpu.VMEM((nb, LANES), f32),
            pltpu.VMEM((nb, LANES), f32),
            pltpu.VMEM((factors * nb, LANES), f32),
            pltpu.VMEM((CHUNKS, 3, per, LANES), f32),
            pltpu.VMEM((3, nb, LANES), f32),
            pltpu.VMEM((CHUNKS, per, LANES), f32),
            pltpu.VMEM((CHUNKS, per, LANES), f32),
            pltpu.VMEM((factors * 8, LANES), f32),
            pltpu.VMEM((factors - 1, 8, LANES), f32),
            pltpu.VMEM((region_n, 6, LANES), f32),
            pltpu.VMEM((region_n, 4, LANES), f32),
            dma((7,)),
            dma((4,)),
            dma((CHUNKS,)),
            dma((CHUNKS,)),
            dma((CHUNKS,)),
            dma((CHUNKS, 3)),
            dma((CHUNKS, 3)),
            dma((3,)),
            dma((3,)),
            dma((CHUNKS,)),
            dma((CHUNKS,)),
            dma((factors - 1,)),
            dma((factors - 1,)),
            dma,
            dma,
            dma,
            dma,
        ],
        compiler_params=pltpu.CompilerParams(
            collective_id=0, has_side_effects=True, vmem_limit_bytes=60 * 2**20
        ),
        cost_estimate=pl.CostEstimate(flops=40_000_000, bytes_accessed=13_000_000, transcendentals=0),
        name="sweep",
    )(
        response,
        loadings.T,
        obs_count.reshape(1, species),
        couplings.reshape(nb, 2).T,
        block_cov.reshape(nb, LANES, LANES),
        noise_factor.reshape(nb, LANES, LANES),
        noise.reshape(nb, LANES),
        latents.reshape(nb, LANES),
        colours,
        partners,
    )
    return out.reshape(1, nb * LANES)


def solution(mesh):
    placed = (
        P("factor", "region"),
        P(),
        P(),
        P("factor", "region", None),
        P("factor", "region", None, None),
        P("factor", "region", None, None),
        P("factor", "region"),
        P("factor", "region"),
        P("region"),
        P("region", None),
    )
    return jax.shard_map(
        on_device, mesh=mesh, in_specs=placed, out_specs=P("factor", "region"), check_vma=False
    )
```

time: 27.8 us -> 26.2 us (0.942)
  Pallas kernels: 26.3 us -> 24.7 us
    pallas_call x1, Pallas kernels: 26.3 us -> 24.7 us  [on_device(): pl.pallas_call(functools.partial(kernel, species), out_shape=jax.ShapeDty...]
where the time goes in v3:
time: 26.2 us; the launch traced here: 26 us
  Pallas kernels  24.7 us (94%)
  local copies, waits for them, and re-layouts  1.38 us (5%)
    pallas_call x1, Pallas kernels, on_device(): pl.pallas_call(functools.partial(kernel, species), out_shape=jax.ShapeDty...  24.7 us
    unnamed x1, local copies, waits for them, and re-layouts  1.38 us

profile of v3, /device:TPU:1, one launch (start us, length us, event | category | flops | bytes accessed | tf_op | source)
XLA Modules:
  0.0 26.0 jit_solution(17613733717942591234)
XLA Ops:
  0.0 24.7 %sweep.1 = f32[64,128]{1,0:T(8,128)} custom-call(bf16[250,8192]{1,0:T(8,128)(2,1)} %resp_hbm.1, f32[8,2000]{1,0:T(8,128)} %bitcast.13, s32[1,2000]{1,0:T(1,128)} %bitcast.16, f32[2,64]{1,0:T(2,128)} %bitcast.17, f32[64,128,128]{2,1,0:T(8,128)} %bitcast.10, f32[64,128,128]{2,1,0:T(8,128)} %bitcast.11, f32[64,128]{1,0:T(8,128)} %bitcast.14, ...), custom_call_target="tpu_custom_call" | custom-call | flops 40000000 | bytes 13000000 | tf_op jit(solution)/shard_map/sweep/pallas_call | solution.py:391
  24.7 1.4 %copy.12 = f32[1,8192]{1,0:T(1,128)} copy(f32[1,8192]{1,0:T(1,128)} %bitcast.12) | data formatting | bytes 65536

commit v4 on v3

--- a/solution.py
+++ b/solution.py
@@ -33,6 +33,8 @@
     coup_v,
     cov_v,
     nf_v,
+    cend_v,
+    nend_v,
     noise_v,
     lat_v,
     col_s,
@@ -53,6 +55,8 @@
     new_v,
     small_sem,
     rend_sem,
+    cend_sem,
+    nend_sem,
     resp_sem,
     nf_sem,
     cov_sem,
@@ -81,6 +85,14 @@
     zi = fi % 2
     end_blocks = (0, half - 1, half, nb - 1)
 
+    x_peers = [lax.rem(xi + d, 4) * 2 for d in (1, 2, 3)]
+    z_peer = xi * 2 + (1 - zi)
+    barrier = pltpu.get_barrier_semaphore()
+    for d in range(1, factors):
+        pl.semaphore_signal(
+            barrier, inc=1, device_id={"factor": lax.rem(fi + d, factors)}, device_id_type=MESH
+        )
+
     small = [
         pltpu.make_async_copy(src, dst, small_sem.at[i])
         for i, (src, dst) in enumerate(
@@ -118,16 +130,12 @@
         ]
         for hbm, ref, sem in ((nf_hbm, nf_v, nf_sem), (cov_hbm, cov_v, cov_sem))
     )
-    for copy in small[:3] + small[5:6] + rend_in + resp_in:
+    cend_in, nend_in = (
+        [pltpu.make_async_copy(hbm.at[b], ref.at[i], sem.at[i]) for i, b in enumerate(end_blocks)]
+        for hbm, ref, sem in ((cov_hbm, cend_v, cend_sem), (nf_hbm, nend_v, nend_sem))
+    )
+    for copy in small[:3] + rend_in:
         copy.start()
-
-    x_peers = [lax.rem(xi + d, 4) * 2 for d in (1, 2, 3)]
-    z_peer = xi * 2 + (1 - zi)
-    barrier = pltpu.get_barrier_semaphore()
-    for d in range(1, factors):
-        pl.semaphore_signal(
-            barrier, inc=1, device_id={"factor": lax.rem(fi + d, factors)}, device_id_type=MESH
-        )
 
     @pl.loop(1, region_n)
     def _(d):
@@ -135,7 +143,7 @@
             barrier, inc=1, device_id={"region": lax.rem(ri + d, region_n)}, device_id_type=MESH
         )
 
-    for copy in small[3:5] + small[6:]:
+    for copy in small[3:] + resp_in[:1] + nend_in + cend_in + resp_in[1:]:
         copy.start()
 
     small[0].wait()
@@ -163,7 +171,8 @@
     term = jnp.dot(mine, rend_v[...], preferred_element_type=jnp.float32)
     for i, b in enumerate(end_blocks):
         value = term[:, i * LANES : (i + 1) * LANES] - gram * lat_v[b : b + 1, :]
-        end_v[pl.ds(i, factors, stride=8), :] = value
+        for k in range(factors):
+            end_v[k, i : i + 1, :] = value[k : k + 1, :]
 
     def send_all(buf, ssem, rsem):
         @pl.loop(1, region_n)
@@ -187,7 +196,7 @@
         peer = lax.rem(fi + d, factors)
         ends_out.append(
             pltpu.make_async_remote_copy(
-                src_ref=end_v.at[pl.ds(pl.multiple_of(peer * 8, 8), 8)],
+                src_ref=end_v.at[peer],
                 dst_ref=end_recv.at[d - 1],
                 send_sem=end_ssem.at[d - 1],
                 recv_sem=end_rsem.at[d - 1],
@@ -304,6 +313,8 @@
         field_v[here, :] = total
 
     def blocks(c):
+        cov_in[c].wait()
+
         @pl.loop(0, per // UNROLL)
         def _(g):
             for k in range(UNROLL):
@@ -319,21 +330,21 @@
         g = par_s[q, side]
         return old_v[g // 2, pl.ds(4 + g % 2, 1), :]
 
+    end_draws = []
+    for i, b in enumerate(end_blocks):
+        nend_in[i].wait()
+        end_draws.append(times(nend_v[i], noise_v[b : b + 1, :]))
     draw(0)
     draw(1)
-    draw(2)
-    for c in range(CHUNKS):
-        x_sum(c)
-    draw(3)
 
     for copy in ends_out:
         copy.wait_recv()
-    own_end = end_v[pl.ds(pl.multiple_of(fi * 8, 8), 8), :]
+    own_end = end_v[fi]
     for d in range(factors - 1):
         own_end = own_end + end_recv[d]
     small[6].wait()
-    for c in range(CHUNKS):
-        cov_in[c].wait()
+    for copy in cend_in:
+        copy.wait()
     wait_all(old_v, old_rsem)
     bases = []
     for i, b in enumerate(end_blocks):
@@ -341,9 +352,13 @@
         bases.append(own_end[i : i + 1, :] + local_v[b : b + 1, :])
         weight = (c0_v, c1_v)[side][b : b + 1, :]
         row = bases[i] + weight * partner_edge(old_v, q, side)
-        new_v[ri, pl.ds(i, 1), :] = times(cov_v[b], row) + draw_v[b : b + 1, :]
+        new_v[ri, pl.ds(i, 1), :] = times(cend_v[i], row) + end_draws[i]
     send_all(new_v, new_ssem, new_rsem)
 
+    for c in range(CHUNKS):
+        x_sum(c)
+    draw(2)
+    draw(3)
     for copy in ys:
         copy.wait_recv()
     for c in range(CHUNKS):
@@ -360,7 +375,7 @@
             partner_edge(old_v, q, side),
         )
         row = bases[i] + weight * edge
-        out_ref[b : b + 1, :] = times(cov_v[b], row) + draw_v[b : b + 1, :]
+        out_ref[b : b + 1, :] = times(cend_v[i], row) + end_draws[i]
 
     for copy in ends_out + ys + zs + [copy for c in range(CHUNKS) for copy in xs[c]]:
         copy.wait_send()
@@ -390,7 +405,7 @@
     dma = pltpu.SemaphoreType.DMA
     out = pl.pallas_call(
         functools.partial(kernel, species),
-        out_shape=jax.ShapeDtypeStruct((nb, LANES), f32),
+        out_shape=pltpu.VMEM((nb, LANES), f32),
         in_specs=[any_spec] * 10,
         out_specs=pl.BlockSpec(memory_space=pltpu.VMEM),
         scratch_shapes=[
@@ -401,6 +416,8 @@
             pltpu.VMEM((2, nb), f32),
             pltpu.VMEM((nb, LANES, LANES), f32),
             pltpu.VMEM((nb, LANES, LANES), f32),
+            pltpu.VMEM((4, LANES, LANES), f32),
+            pltpu.VMEM((4, LANES, LANES), f32),
             pltpu.VMEM((nb, LANES), f32),
             pltpu.VMEM((nb, LANES), f32),
             pltpu.SMEM((2,), jnp.int32),
@@ -415,11 +432,13 @@
             pltpu.VMEM((3, nb, LANES), f32),
             pltpu.VMEM((CHUNKS, per, LANES), f32),
             pltpu.VMEM((CHUNKS, per, LANES), f32),
-            pltpu.VMEM((factors * 8, LANES), f32),
-            pltpu.VMEM((factors - 1, 8, LANES), f32),
+            pltpu.VMEM((factors, 4, LANES), f32),
+            pltpu.VMEM((factors - 1, 4, LANES), f32),
             pltpu.VMEM((region_n, 6, LANES), f32),
             pltpu.VMEM((region_n, 4, LANES), f32),
             dma((7,)),
+            dma((4,)),
+            dma((4,)),
             dma((4,)),
             dma((CHUNKS,)),
             dma((CHUNKS,)),

time: 26.2 us -> 24 us (0.916)
  Pallas kernels: 24.7 us -> 23.3 us
  local copies, waits for them, and re-layouts: 1.38 us -> 0.62 us
    pallas_call x1, Pallas kernels: 24.7 us -> 23.3 us  [on_device(): pl.pallas_call(functools.partial(kernel, species), out_shape=pltpu.VMEM((...]
    unnamed x1, local copies, waits for them, and re-layouts: 1.38 us -> 0.62 us
where the time goes in v4:
time: 24 us; the launch traced here: 23.9 us
  Pallas kernels  23.3 us (97%)
  local copies, waits for them, and re-layouts  0.62 us (3%)
    pallas_call x1, Pallas kernels, on_device(): pl.pallas_call(functools.partial(kernel, species), out_shape=pltpu.VMEM((...  23.3 us
    unnamed x1, local copies, waits for them, and re-layouts  0.62 us

profile of v4, /device:TPU:1, one launch (start us, length us, event | category | flops | bytes accessed | tf_op | source)
XLA Modules:
  0.0 23.9 jit_solution(2739769003092442013)
XLA Ops:
  0.0 23.3 %sweep.1 = f32[64,128]{1,0:T(8,128)S(1)} custom-call(bf16[250,8192]{1,0:T(8,128)(2,1)} %resp_hbm.1, f32[8,2000]{1,0:T(8,128)} %bitcast.13, s32[1,2000]{1,0:T(1,128)} %bitcast.16, f32[2,64]{1,0:T(2,128)} %bitcast.17, f32[64,128,128]{2,1,0:T(8,128)} %bitcast.11, f32[64,128,128]{2,1,0:T(8,128)} %bitcast.12, f32[64,128]{1,0:T(8,128)} %bitcast.14, ...), custom_call_target="tpu_custom_call" | custom-call | flops 40000000 | bytes 13000000 | tf_op jit(solution)/shard_map/sweep/pallas_call | solution.py:406
  23.3 0.6 %copy.12 = f32[1,8192]{1,0:T(1,128)} copy(f32[1,8192]{1,0:T(1,128)S(1)} %bitcast.10) | data formatting | bytes 65536

commit v5 on v4

--- a/solution.py
+++ b/solution.py
@@ -175,8 +175,7 @@
             end_v[k, i : i + 1, :] = value[k : k + 1, :]
 
     def send_all(buf, ssem, rsem):
-        @pl.loop(1, region_n)
-        def _(d):
+        for d in sorted(range(1, region_n), key=lambda d: abs(d - region_n // 2)):
             pltpu.make_async_remote_copy(
                 src_ref=buf.at[ri],
                 dst_ref=buf.at[ri],
@@ -192,8 +191,8 @@
 
     pl.semaphore_wait(barrier, factors - 1 + region_n - 1)
     ends_out = []
-    for d in range(1, factors):
-        peer = lax.rem(fi + d, factors)
+    ends_to = [x_peers[d] + 1 - zi for d in (1, 0, 2)] + [z_peer] + [p + zi for p in x_peers]
+    for d, peer in enumerate(ends_to, 1):
         ends_out.append(
             pltpu.make_async_remote_copy(
                 src_ref=end_v.at[peer],
@@ -336,6 +335,8 @@
         end_draws.append(times(nend_v[i], noise_v[b : b + 1, :]))
     draw(0)
     draw(1)
+    for c in range(CHUNKS):
+        x_sum(c)
 
     for copy in ends_out:
         copy.wait_recv()
@@ -355,8 +356,6 @@
         new_v[ri, pl.ds(i, 1), :] = times(cend_v[i], row) + end_draws[i]
     send_all(new_v, new_ssem, new_rsem)
 
-    for c in range(CHUNKS):
-        x_sum(c)
     draw(2)
     draw(3)
     for copy in ys:

time: 24 us -> 23.9 us (level)
  no operation moved by 1% of the time
where the time goes in v5:
time: 23.9 us; the launch traced here: 23.8 us
  Pallas kernels  23.2 us (97%)
  local copies, waits for them, and re-layouts  0.62 us (3%)
    pallas_call x1, Pallas kernels, on_device(): pl.pallas_call(functools.partial(kernel, species), out_shape=pltpu.VMEM((...  23.2 us
    unnamed x1, local copies, waits for them, and re-layouts  0.62 us

profile of v5, /device:TPU:1, one launch (start us, length us, event | category | flops | bytes accessed | tf_op | source)
XLA Modules:
  0.0 23.8 jit_solution(8962311750702863298)
XLA Ops:
  0.0 23.2 %sweep.1 = f32[64,128]{1,0:T(8,128)S(1)} custom-call(bf16[250,8192]{1,0:T(8,128)(2,1)} %resp_hbm.1, f32[8,2000]{1,0:T(8,128)} %bitcast.13, s32[1,2000]{1,0:T(1,128)} %bitcast.16, f32[2,64]{1,0:T(2,128)} %bitcast.17, f32[64,128,128]{2,1,0:T(8,128)} %bitcast.11, f32[64,128,128]{2,1,0:T(8,128)} %bitcast.12, f32[64,128]{1,0:T(8,128)} %bitcast.14, ...), custom_call_target="tpu_custom_call" | custom-call | flops 40000000 | bytes 13000000 | tf_op jit(solution)/shard_map/sweep/pallas_call | solution.py:405
  23.2 0.6 %copy.12 = f32[1,8192]{1,0:T(1,128)} copy(f32[1,8192]{1,0:T(1,128)S(1)} %bitcast.10) | data formatting | bytes 65536

commit v6 on v5

--- a/solution.py
+++ b/solution.py
@@ -338,21 +338,24 @@
     for c in range(CHUNKS):
         x_sum(c)
 
-    for copy in ends_out:
-        copy.wait_recv()
-    own_end = end_v[fi]
-    for d in range(factors - 1):
-        own_end = own_end + end_recv[d]
     small[6].wait()
     for copy in cend_in:
         copy.wait()
     wait_all(old_v, old_rsem)
+    old_ends, weights = [], []
+    for i, b in enumerate(end_blocks):
+        q, side = i // 2, i % 2
+        old_ends.append(partner_edge(old_v, q, side))
+        weights.append((c0_v, c1_v)[side][b : b + 1, :])
+    own_end = end_v[fi]
+    for copy in ends_out:
+        copy.wait_recv()
+    for d in range(factors - 1):
+        own_end = own_end + end_recv[d]
     bases = []
     for i, b in enumerate(end_blocks):
-        q, side = i // 2, i % 2
         bases.append(own_end[i : i + 1, :] + local_v[b : b + 1, :])
-        weight = (c0_v, c1_v)[side][b : b + 1, :]
-        row = bases[i] + weight * partner_edge(old_v, q, side)
+        row = bases[i] + weights[i] * old_ends[i]
         new_v[ri, pl.ds(i, 1), :] = times(cend_v[i], row) + end_draws[i]
     send_all(new_v, new_ssem, new_rsem)
 
@@ -363,23 +366,21 @@
     for c in range(CHUNKS):
         z_sum(c)
         blocks(c)
-    wait_all(new_v, new_rsem)
-    for i, b in enumerate(end_blocks):
-        q, side = i // 2, i % 2
-        weight = (c0_v, c1_v)[side][b : b + 1, :]
-        own = jnp.full((1, LANES), col_s[q].astype(jnp.float32))
-        edge = jnp.where(
-            partner_colour(q, side) < own,
-            partner_edge(new_v, q, side),
-            partner_edge(old_v, q, side),
-        )
-        row = bases[i] + weight * edge
-        out_ref[b : b + 1, :] = times(cend_v[i], row) + end_draws[i]
-
     for copy in ends_out + ys + zs + [copy for c in range(CHUNKS) for copy in xs[c]]:
         copy.wait_send()
     wait_all(old_v, old_ssem)
     wait_all(new_v, new_ssem)
+    later = []
+    for i, b in enumerate(end_blocks):
+        q, side = i // 2, i % 2
+        own = jnp.full((1, LANES), col_s[q].astype(jnp.float32))
+        later.append(partner_colour(q, side) < own)
+    wait_all(new_v, new_rsem)
+    for i, b in enumerate(end_blocks):
+        q, side = i // 2, i % 2
+        edge = jnp.where(later[i], partner_edge(new_v, q, side), old_ends[i])
+        row = bases[i] + weights[i] * edge
+        out_ref[b : b + 1, :] = times(cend_v[i], row) + end_draws[i]
 
 
 def on_device(
@@ -426,7 +427,7 @@
             pltpu.VMEM((nb, LANES), f32),
             pltpu.VMEM((nb, LANES), f32),
             pltpu.VMEM((nb, LANES), f32),
-            pltpu.VMEM((factors * nb, LANES), f32),
+            pltpu.VMEM(((factors + 1) * nb, LANES), f32),
             pltpu.VMEM((CHUNKS, 3, per, LANES), f32),
             pltpu.VMEM((3, nb, LANES), f32),
             pltpu.VMEM((CHUNKS, per, LANES), f32),

time: 23.9 us -> 23.8 us (level)
  no operation moved by 1% of the time
where the time goes in v6:
time: 23.8 us; the launch traced here: 23.7 us
  Pallas kernels  23.1 us (97%)
  local copies, waits for them, and re-layouts  0.62 us (3%)
    pallas_call x1, Pallas kernels, on_device(): pl.pallas_call(functools.partial(kernel, species), out_shape=pltpu.VMEM((...  23.1 us
    unnamed x1, local copies, waits for them, and re-layouts  0.62 us

profile of v6, /device:TPU:1, one launch (start us, length us, event | category | flops | bytes accessed | tf_op | source)
XLA Modules:
  0.0 23.7 jit_solution(16720911729549958148)
XLA Ops:
  0.0 23.1 %sweep.1 = f32[64,128]{1,0:T(8,128)S(1)} custom-call(bf16[250,8192]{1,0:T(8,128)(2,1)} %resp_hbm.1, f32[8,2000]{1,0:T(8,128)} %bitcast.13, s32[1,2000]{1,0:T(1,128)} %bitcast.16, f32[2,64]{1,0:T(2,128)} %bitcast.17, f32[64,128,128]{2,1,0:T(8,128)} %bitcast.11, f32[64,128,128]{2,1,0:T(8,128)} %bitcast.12, f32[64,128]{1,0:T(8,128)} %bitcast.14, ...), custom_call_target="tpu_custom_call" | custom-call | flops 40000000 | bytes 13000000 | tf_op jit(solution)/shard_map/sweep/pallas_call | solution.py:406
  23.1 0.6 %copy.12 = f32[1,8192]{1,0:T(1,128)} copy(f32[1,8192]{1,0:T(1,128)S(1)} %bitcast.10) | data formatting | bytes 65536

commit v7 on v6

--- a/solution.py
+++ b/solution.py
@@ -256,8 +256,6 @@
             part_v[pl.ds(b, factors, stride=nb), :] = value
         for copy in xs[c]:
             copy.start()
-    for copy in ys:
-        copy.start()
 
     diagonal = lax.broadcasted_iota(jnp.int32, (LANES, LANES), 0) == lax.broadcasted_iota(
         jnp.int32, (LANES, LANES), 1
@@ -335,6 +333,8 @@
         end_draws.append(times(nend_v[i], noise_v[b : b + 1, :]))
     draw(0)
     draw(1)
+    for copy in ys:
+        copy.start()
     for c in range(CHUNKS):
         x_sum(c)
 

time: 23.8 us -> 23.7 us (level)
  no operation moved by 1% of the time
where the time goes in v7:
time: 23.7 us
  Pallas kernels  23 us (97%)
  local copies, waits for them, and re-layouts  0.62 us (3%)
    pallas_call x1, Pallas kernels, on_device(): pl.pallas_call(functools.partial(kernel, species), out_shape=pltpu.VMEM((...  23 us
    unnamed x1, local copies, waits for them, and re-layouts  0.62 us

profile of v7, /device:TPU:1, one launch (start us, length us, event | category | flops | bytes accessed | tf_op | source)
XLA Modules:
  0.0 23.7 jit_solution(192109204512493247)
XLA Ops:
  0.0 23.0 %sweep.1 = f32[64,128]{1,0:T(8,128)S(1)} custom-call(bf16[250,8192]{1,0:T(8,128)(2,1)} %resp_hbm.1, f32[8,2000]{1,0:T(8,128)} %bitcast.13, s32[1,2000]{1,0:T(1,128)} %bitcast.16, f32[2,64]{1,0:T(2,128)} %bitcast.17, f32[64,128,128]{2,1,0:T(8,128)} %bitcast.11, f32[64,128,128]{2,1,0:T(8,128)} %bitcast.12, f32[64,128]{1,0:T(8,128)} %bitcast.14, ...), custom_call_target="tpu_custom_call" | custom-call | flops 40000000 | bytes 13000000 | tf_op jit(solution)/shard_map/sweep/pallas_call | solution.py:406
  23.0 0.6 %copy.12 = f32[1,8192]{1,0:T(1,128)} copy(f32[1,8192]{1,0:T(1,128)S(1)} %bitcast.10) | data formatting | bytes 65536

commit v8 on v6

--- a/solution.py
+++ b/solution.py
@@ -189,6 +189,21 @@
         others = buf.at[pl.ds(0, region_n - 1)]
         pltpu.make_async_copy(others, others, sem).wait()
 
+    small[3].wait()
+    pick = lax.broadcasted_iota(jnp.int32, (nb, nb), 0) == lax.broadcasted_iota(
+        jnp.int32, (nb, nb), 1
+    )
+    for i, ref in ((0, c0_v), (1, c1_v)):
+        column = jnp.sum(jnp.where(pick, coup_v[i : i + 1, :], 0.0), axis=1, keepdims=True)
+        ref[...] = jnp.broadcast_to(column, (nb, LANES))
+    rows_at = lax.broadcasted_iota(jnp.int32, (nb, LANES), 0)
+    left = pltpu.roll(lat_v[...], 1, 0)
+    left = jnp.where((rows_at == 0) | (rows_at == half), 0.0, left)
+    right = pltpu.roll(lat_v[...], nb - 1, 0)
+    right = jnp.where((rows_at == half - 1) | (rows_at == nb - 1), 0.0, right)
+    local_v[...] = c0_v[...] * left + c1_v[...] * right
+    small[4].wait()
+
     pl.semaphore_wait(barrier, factors - 1 + region_n - 1)
     ends_out = []
     ends_to = [x_peers[d] + 1 - zi for d in (1, 0, 2)] + [z_peer] + [p + zi for p in x_peers]
@@ -266,21 +281,6 @@
     def times(matrix, row):
         sums = jnp.sum(matrix * row, axis=1, keepdims=True)
         return jnp.sum(jnp.where(diagonal, sums, 0.0), axis=0, keepdims=True)
-
-    small[3].wait()
-    pick = lax.broadcasted_iota(jnp.int32, (nb, nb), 0) == lax.broadcasted_iota(
-        jnp.int32, (nb, nb), 1
-    )
-    for i, ref in ((0, c0_v), (1, c1_v)):
-        column = jnp.sum(jnp.where(pick, coup_v[i : i + 1, :], 0.0), axis=1, keepdims=True)
-        ref[...] = jnp.broadcast_to(column, (nb, LANES))
-    rows_at = lax.broadcasted_iota(jnp.int32, (nb, LANES), 0)
-    left = pltpu.roll(lat_v[...], 1, 0)
-    left = jnp.where((rows_at == 0) | (rows_at == half), 0.0, left)
-    right = pltpu.roll(lat_v[...], nb - 1, 0)
-    right = jnp.where((rows_at == half - 1) | (rows_at == nb - 1), 0.0, right)
-    local_v[...] = c0_v[...] * left + c1_v[...] * right
-    small[4].wait()
 
     UNROLL = 8
 

time: 23.8 us -> 23.8 us (level)
  no operation moved by 1% of the time
where the time goes in v8:
time: 23.8 us; the launch traced here: 23.7 us
  Pallas kernels  23.1 us (97%)
  local copies, waits for them, and re-layouts  0.62 us (3%)
    pallas_call x1, Pallas kernels, on_device(): pl.pallas_call(functools.partial(kernel, species), out_shape=pltpu.VMEM((...  23.1 us
    unnamed x1, local copies, waits for them, and re-layouts  0.62 us

profile of v8, /device:TPU:1, one launch (start us, length us, event | category | flops | bytes accessed | tf_op | source)
XLA Modules:
  0.0 23.7 jit_solution(6673730920333734652)
XLA Ops:
  0.0 23.1 %sweep.1 = f32[64,128]{1,0:T(8,128)S(1)} custom-call(bf16[250,8192]{1,0:T(8,128)(2,1)} %resp_hbm.1, f32[8,2000]{1,0:T(8,128)} %bitcast.13, s32[1,2000]{1,0:T(1,128)} %bitcast.16, f32[2,64]{1,0:T(2,128)} %bitcast.17, f32[64,128,128]{2,1,0:T(8,128)} %bitcast.11, f32[64,128,128]{2,1,0:T(8,128)} %bitcast.12, f32[64,128]{1,0:T(8,128)} %bitcast.14, ...), custom_call_target="tpu_custom_call" | custom-call | flops 40000000 | bytes 13000000 | tf_op jit(solution)/shard_map/sweep/pallas_call | solution.py:406
  23.1 0.6 %copy.12 = f32[1,8192]{1,0:T(1,128)} copy(f32[1,8192]{1,0:T(1,128)S(1)} %bitcast.10) | data formatting | bytes 65536
